TPU v7x, 32 devices: a whole 2x2x4 slice. The times are simulated.
32 devices in a mesh: slab: 8 (over z, x), leaf: 4 (over y, core).
Axes of the slice: x: 2, y: 2, z: 4, core: 2. Of those that a mesh axis runs over, the one named last changes fastest.
Arguments:
- particles: float32 [3, 32, 16, 256], P(None, 'slab', 'leaf'), may hold values from -1.05 to 1.05, as said below
- near_mask: int32 [16, 32, 16], P(None, 'slab', 'leaf'), may hold values from 0 to 1, as said below
Outputs:
- velocity: float32 [2, 32, 16, 256], P(None, 'slab', 'leaf')
Inputs may be any that keep to these rules, and one draw needn't show every extreme that they name: `particles`: entries 0 and 1 of the first dimension are offsets; entry 2 is the circulation. near_mask[o, i, j] = near_mask[15 - o, i + dx, j + dy], where (dx, dy) is step o of the 16 steps with max(|dx|, |dy|) = 2 in row-major order over dx, then dy; it is 0 where leaf (i + dx, j + dy) lies outside the grid.
All inputs are finite; a program needn't handle non-finite values.
Results may differ from a plain program's by a relative error of at most 0.0003.
Values sent between devices are 32-bit elements; how exact they have to be, the bound alone decides.
A program may use at most 64 MiB of HBM per device.

v0:
```python
import functools
import math

import jax
import jax.numpy as jnp
import numpy as np
from jax import lax
from jax.experimental import pallas as pl
from jax.experimental.pallas import tpu as pltpu
from jax.sharding import PartitionSpec as P

ORDER = 10
DELTA_SQUARED = 0.0025
TWO_PI = 2.0 * math.pi
MESH = pl.DeviceIdType.MESH
CYCLE = [(a, b) for a in range(-2, 3) for b in range(-2, 3) if max(abs(a), abs(b)) == 2]
DIRECTIONS = [(a, b) for a in (-1, 0, 1) for b in (-1, 0, 1) if (a, b) != (0, 0)]
WIDTH = 2
FEATURES = 48
CHUNK = 128
MULTI = 24


def span(step, side):
    return {-1: (0, WIDTH), 0: (0, side), 1: (side - WIDTH, WIDTH)}[step]


def landing(step, side):
    return {1: 0, 0: WIDTH, -1: WIDTH + side}[step]


def moment_columns(base_x, base_y, strength, lane):
    power_x, power_y = strength, jnp.zeros_like(strength)
    out = jnp.zeros(lane.shape, jnp.float32)
    for k in range(ORDER):
        if k:
            power_x, power_y = (
                power_x * base_x - power_y * base_y,
                power_x * base_y + power_y * base_x,
            )
        out = jnp.where(lane == k, jnp.sum(power_x, axis=1, keepdims=True), out)
        if k:
            out = jnp.where(lane == ORDER + k, jnp.sum(power_y, axis=1, keepdims=True), out)
    return out


def rounded(values):
    return values.astype(jnp.bfloat16).astype(jnp.float32)


def pieces(value, place, extra):
    coarse = jnp.floor(value * 32.0 + 0.5) * (1.0 / 32.0)
    rest = value - coarse
    rest_1 = rounded(rest)
    rest_2 = rounded(rest - rest_1)
    rest = rest_1 + rest_2
    coarse = coarse + place
    square = coarse * coarse
    square_1 = rounded(square)
    square_2 = square - square_1
    cross = 2.0 * coarse * rest + (rest * rest + extra)
    cross_1 = rounded(cross)
    cross_2 = rounded(cross - cross_1)
    cross_3 = cross - cross_1 - cross_2
    return dict(
        one=jnp.ones_like(value), h=coarse, l1=rest_1, l2=rest_2, s1=square_1, s2=square_2,
        c1=cross_1, c2=cross_2, c3=cross_3,
    )


HIGH = [
    ("s1", 1.0, "one"), ("s2", 1.0, "one"), ("one", 1.0, "s1"), ("one", 1.0, "s2"),
    ("h", -2.0, "h"),
]
LOW = [
    ("c1", 1.0, "one"), ("c2", 1.0, "one"), ("c3", 1.0, "one"),
    ("one", 1.0, "c1"), ("one", 1.0, "c2"), ("one", 1.0, "c3"),
    ("h", -2.0, "l1"), ("h", -2.0, "l2"), ("l1", -2.0, "h"), ("l2", -2.0, "h"),
    ("l1", -2.0, "l1"), ("l1", -2.0, "l2"), ("l2", -2.0, "l1"),
]
ROWS = [(axis, row) for rows in (HIGH, LOW) for axis in (0, 1) for row in rows]


def field_kernel(slabs, leaves, side, mask_ref, part_ref, out_ref, *refs):
    win_ref, own_ref, near_ref, block_ref = refs[:4]
    sends, recvs = refs[4:12], refs[12:20]
    multi_ref, row_ref = refs[20:22]
    halo_send, halo_recv, multi_send, multi_recv, row_send, row_recv = refs[22:28]
    source_ref, target_ref, left_ref, right_ref, gain_ref, acc_ref, sum_ref = refs[28:]
    count = slabs * leaves
    window = side + 2 * WIDTH
    own = side * side
    particles = part_ref.shape[3]
    halves = particles // 128
    all_leaves = window * window
    slab, leaf = lax.axis_index("slab"), lax.axis_index("leaf")
    me = slab * leaves + leaf

    def place(number):
        return (number // leaves, lax.rem(number, leaves))

    barrier = pltpu.get_barrier_semaphore()

    @pl.loop(1, count)
    def _(o):
        pl.semaphore_signal(
            barrier, inc=1, device_id=place(lax.rem(me + o, count)), device_id_type=MESH
        )

    for c in range(3):
        for i in range(side):
            own_ref[c, i * side : (i + 1) * side, :] = part_ref[c, i]
    win_ref[...] = jnp.zeros_like(win_ref)
    for c in range(3):
        for i in range(side):
            at = (i + WIDTH) * window + WIDTH
            win_ref[c, at : at + side, :] = part_ref[c, i]
    for k, (a, b) in enumerate(DIRECTIONS):
        (i0, ni), (j0, nj) = span(a, side), span(b, side)
        for c in range(3):
            for r in range(ni):
                sends[k][c, r * nj : (r + 1) * nj, :] = part_ref[c, i0 + r, j0 : j0 + nj, :]

    def exists(a, b):
        s, l = slab + a, leaf + b
        return (s >= 0) & (s < slabs) & (l >= 0) & (l < leaves)

    def halo_copy(k):
        a, b = DIRECTIONS[k]
        return pltpu.make_async_remote_copy(
            src_ref=sends[k], dst_ref=recvs[k],
            send_sem=halo_send.at[k], recv_sem=halo_recv.at[k],
            device_id=(slab + a, leaf + b), device_id_type=MESH,
        )

    def multi_copy(k):
        a, b = DIRECTIONS[k]
        return pltpu.make_async_remote_copy(
            src_ref=multi_ref, dst_ref=near_ref.at[(1 - a) * 3 + (1 - b)],
            send_sem=multi_send.at[k], recv_sem=multi_recv.at[k],
            device_id=(slab + a, leaf + b), device_id_type=MESH,
        )

    def row_copy(o):
        return pltpu.make_async_remote_copy(
            src_ref=row_ref, dst_ref=block_ref.at[me],
            send_sem=row_send.at[o], recv_sem=row_recv.at[o],
            device_id=place(lax.rem(me + o, count)), device_id_type=MESH,
        )

    pl.semaphore_wait(barrier, count - 1)
    for k, (a, b) in enumerate(DIRECTIONS):
        @pl.when(exists(a, b))
        def _(k=k):
            halo_copy(k).start()

    own_x, own_y, strength = own_ref[0], own_ref[1], own_ref[2]
    lane = lax.broadcasted_iota(jnp.int32, (side * side, 128), 1)
    number = lax.broadcasted_iota(jnp.int32, own_x.shape, 0)
    centred_x = (number // side).astype(jnp.float32) - (side - 1) / 2.0
    centred_y = (number % side).astype(jnp.float32) - (side - 1) / 2.0
    block = moment_columns(own_x + centred_x, own_y + centred_y, strength, lane)
    row_ref[...] = jnp.sum(block, axis=0, keepdims=True)
    block_ref[me] = row_ref[...]

    @pl.loop(1, count)
    def _(o):
        row_copy(o).start()

    columns = moment_columns(own_x, own_y, strength, lane)
    square = jnp.concatenate(
        [columns, jnp.zeros((128 - side * side, 128), jnp.float32)], axis=0
    )
    multi_ref[...] = square.T[:MULTI]
    near_ref[4] = multi_ref[...]
    for k, (a, b) in enumerate(DIRECTIONS):
        @pl.when(exists(a, b))
        def _(k=k):
            multi_copy(k).start()

        @pl.when(jnp.logical_not(exists(-a, -b)))
        def _(a=a, b=b):
            near_ref[(1 - a) * 3 + (1 - b)] = jnp.zeros((MULTI, 128), jnp.float32)

    def fill(ref, get, width, is_target, groups):
        leaf_count = width * width
        stride = leaf_count + 8
        index = lax.broadcasted_iota(jnp.int32, (8, 128), 0)
        low = 0 if is_target else WIDTH
        for g in groups:
            place_x = ((index + g * 8) // width - low).astype(jnp.float32) - (side - 1) / 2.0
            place_y = ((index + g * 8) % width - low).astype(jnp.float32) - (side - 1) / 2.0
            for half in range(halves):
                lanes = slice(half * 128, (half + 1) * 128)
                extra = DELTA_SQUARED / 2.0 if is_target else 0.0
                parts = [
                    pieces(get(c, g, lanes), place, extra)
                    for c, place in ((0, place_x), (1, place_y))
                ]
                for r in range(FEATURES):
                    if r < len(ROWS):
                        axis, (target, factor, source) = ROWS[r]
                        value = parts[axis][target] * factor if is_target else parts[axis][source]
                    else:
                        value = jnp.zeros((8, 128), jnp.float32)
                    ref[half, r * stride + g * 8 : r * stride + g * 8 + 8, :] = value


    def target_leaf(t):
        for half in range(halves):
            rows = target_ref[half, pl.ds(t, FEATURES, stride=own + 8), :]
            left_ref[half * 128 : (half + 1) * 128, :] = rows.T.astype(jnp.bfloat16)

    def source_leaf(number):
        for half in range(halves):
            lanes = slice(half * 128, (half + 1) * 128)
            rows = source_ref[half, pl.ds(number, FEATURES, stride=all_leaves + 8), :]
            right_ref[number, :, lanes] = rows.astype(jnp.bfloat16)

    def pair_sums(t, ti, tj, steps, first):
        target_leaf(t)
        sources = []
        for number, (dx, dy) in enumerate(steps):
            source = (ti + (dx + WIDTH)) * window + tj + (dy + WIDTH)
            sources.append(source)
            strength = win_ref[2, pl.ds(source, 1), :]
            if isinstance(dx, int) and isinstance(dy, int):
                if max(abs(dx), abs(dy)) == 2:
                    o = CYCLE.index((dx, dy))
                    strength = strength * mask_ref[o, ti, tj].astype(jnp.float32)
                shift_x, shift_y = float(dx), float(dy)
            else:
                dx, dy = jnp.int32(dx), jnp.int32(dy)
                o = jnp.where(dx == -2, dy + 2, jnp.where(dx == 2, dy + 13, 7 + 2 * dx))
                o = jnp.where((jnp.abs(dx) < 2) & (dy == 2), o + 1, o)
                o = jnp.maximum(0, jnp.minimum(o, len(CYCLE) - 1))
                outer = jnp.maximum(jnp.abs(dx), jnp.abs(dy)) == 2
                chosen = jnp.where(outer, mask_ref[o, ti, tj], 1)
                strength = strength * chosen.astype(jnp.float32)
                shift_x, shift_y = dx.astype(jnp.float32), dy.astype(jnp.float32)
            gain_ref[number, 0:1, :] = strength
            gain_ref[number, 1:2, :] = strength * (win_ref[0, pl.ds(source, 1), :] + shift_x)
            gain_ref[number, 2:3, :] = strength * (win_ref[1, pl.ds(source, 1), :] + shift_y)

        @pl.loop(0, particles // CHUNK)
        def _(chunk):
            at = pl.multiple_of(chunk * CHUNK, CHUNK)
            left = left_ref[pl.ds(at, CHUNK), :]
            totals = [jnp.zeros((CHUNK, 128), jnp.float32) for _ in range(3)]
            for number, source in enumerate(sources):
                distance = jnp.dot(left, right_ref[source], preferred_element_type=jnp.float32)
                inverse = pl.reciprocal(distance, approx=True)
                for half in range(halves):
                    lanes = slice(half * 128, (half + 1) * 128)
                    part = inverse[:, lanes]
                    for q in range(3):
                        totals[q] = totals[q] + part * gain_ref[number, q : q + 1, lanes]
            for q in range(3):
                acc_ref[q, pl.ds(at, CHUNK), :] = totals[q]

        for q in range(3):
            sums = jnp.concatenate(
                [
                    jnp.sum(acc_ref[q, half * 128 : (half + 1) * 128, :].T, axis=0, keepdims=True)
                    for half in range(halves)
                ],
                axis=1,
            )
            if first:
                sum_ref[q, pl.ds(t, 1), :] = sums
            else:
                sum_ref[q, pl.ds(t, 1), :] = sum_ref[q, pl.ds(t, 1), :] + sums

    def own_rows(c, g, lanes):
        return own_ref[c, g * 8 : g * 8 + 8, lanes]

    def window_rows(c, g, lanes):
        return win_ref[c, g * 8 : g * 8 + 8, lanes]

    fill(target_ref, own_rows, side, True, range(own // 8))
    fill(source_ref, window_rows, window, False, range(WIDTH, WIDTH + side))

    @pl.loop(0, own)
    def _(s):
        source_leaf((s // side + WIDTH) * window + lax.rem(s, side) + WIDTH)

    inner_side = 2 * WIDTH + 2 - side
    inner_low = side - 1 - WIDTH

    @pl.loop(0, inner_side * inner_side)
    def _(n):
        ti, tj = inner_low + n // inner_side, inner_low + lax.rem(n, inner_side)
        steps = [(si - ti, sj - tj) for si in range(side) for sj in range(side)]
        pair_sums(ti * side + tj, ti, tj, steps, True)

    for k, (a, b) in enumerate(DIRECTIONS):
        @pl.when(exists(-a, -b))
        def _(k=k, a=a, b=b):
            halo_copy(k).wait_recv()
            (i0, ni), (j0, nj) = span(a, side), span(b, side)
            for c in range(3):
                for r in range(ni):
                    at = (landing(a, side) + r) * window + landing(b, side)
                    win_ref[c, at : at + nj, :] = recvs[k][c, r * nj : (r + 1) * nj, :]
            multi_copy(k).wait_recv()

        @pl.when(exists(a, b))
        def _(k=k):
            halo_copy(k).wait_send()
            multi_copy(k).wait_send()

    @pl.loop(1, count)
    def _(o):
        row_copy(o).wait_recv()
        row_copy(o).wait_send()


    fill(source_ref, window_rows, window, False, range(all_leaves // 8))

    @pl.loop(0, all_leaves)
    def _(s):
        source_leaf(s)

    @pl.loop(0, inner_side * inner_side)
    def _(n):
        ti, tj = inner_low + n // inner_side, inner_low + lax.rem(n, inner_side)
        out_x = jnp.where(ti == inner_low, -WIDTH, WIDTH)
        out_y = jnp.where(tj == inner_low, -WIDTH, WIDTH)
        steps = [(out_x, dy) for dy in range(-WIDTH, WIDTH + 1)]
        steps += [(si - ti, out_y) for si in range(side)]
        pair_sums(ti * side + tj, ti, tj, steps, False)

    edge = own - inner_side * inner_side

    @pl.loop(0, edge)
    def _(n):
        t = jnp.where(n < side, n, jnp.where(n >= edge - side, n + own - edge, 0))
        turn = n - side
        between = (turn // 2 + 1) * side + lax.rem(turn, 2) * (side - 1)
        t = jnp.where((n >= side) & (n < edge - side), between, t)
        steps = [(dx, dy) for dx in range(-WIDTH, WIDTH + 1) for dy in range(-WIDTH, WIDTH + 1)]
        pair_sums(t, t // side, lax.rem(t, side), steps, True)

    in_window = 9 * own
    rows = block_ref[:, 0, :]
    block_lanes = -(-count // 128) * 128
    if block_lanes > count:
        rows = jnp.concatenate(
            [rows, jnp.zeros((block_lanes - count, 128), jnp.float32)], axis=0
        )
    blocks = jnp.concatenate(
        [rows[k * 128 : (k + 1) * 128].T[:MULTI] for k in range(block_lanes // 128)], axis=1
    )
    near_lane = lax.broadcasted_iota(jnp.int32, (MULTI, 128), 1)
    groups = -(-in_window // 128)
    parts = [jnp.zeros((MULTI, 128), jnp.float32) for _ in range(groups)]
    for d in range(9):
        piece = jnp.where(near_lane < own, near_ref[d], 0.0)
        at = d * own
        shift = at % 128
        if shift:
            piece = pltpu.roll(piece, shift, 1)
        parts[at // 128] = parts[at // 128] + piece
    used = in_window % 128
    if used and used + count <= 128:
        first_block = in_window
        parts[-1] = parts[-1] + pltpu.roll(blocks[:, :128], used, 1)
    else:
        first_block = groups * 128
        parts.append(blocks)
    moments = jnp.concatenate(parts, axis=1)
    total_lanes = moments.shape[1]

    lane = lax.broadcasted_iota(jnp.int32, (own, total_lanes), 1)
    row = lax.broadcasted_iota(jnp.int32, (own, total_lanes), 0)
    ti, tj = row // side, row % side
    device = lane // own
    inside = lane % own
    dx = (device // 3 - 1) * side + inside // side - ti
    dy = (device % 3 - 1) * side + inside % side - tj
    reach = jnp.maximum(jnp.abs(dx), jnp.abs(dy))
    weight = jnp.zeros((own, total_lanes), jnp.float32)
    for o, (a, b) in enumerate(CYCLE):
        column = jnp.zeros((own, total_lanes), jnp.float32)
        for t in range(own):
            kept = 1.0 - mask_ref[o, t // side, t % side].astype(jnp.float32)
            column = jnp.where(row == t, kept, column)
        weight = jnp.where((dx == a) & (dy == b), column, weight)
    weight = jnp.where(reach >= 3, 1.0, weight)
    weight = jnp.where(lane < in_window, weight, 0.0)
    number = lane - first_block
    block_x, block_y = number // leaves, number % leaves
    remote = (number >= 0) & (number < count) & (
        jnp.maximum(jnp.abs(block_x - slab), jnp.abs(block_y - leaf)) >= 2
    )
    middle = (side - 1) / 2.0
    far_x = ((block_x - slab) * side - ti).astype(jnp.float32) + middle
    far_y = ((block_y - leaf) * side - tj).astype(jnp.float32) + middle
    weight = jnp.where(remote, 1.0, weight)
    shift_x = jnp.where(remote, far_x, dx.astype(jnp.float32))
    shift_y = jnp.where(remote, far_y, dy.astype(jnp.float32))
    shift_x = jnp.where(weight == 0.0, 1.0, shift_x)
    shift_y = jnp.where(weight == 0.0, 0.0, shift_y)
    denominator = shift_x * shift_x + shift_y * shift_y
    base_x, base_y = shift_x / denominator, -shift_y / denominator
    power_x, power_y = [weight * base_x], [weight * base_y]
    for n in range(1, 2 * ORDER - 1):
        last_x, last_y = power_x[-1] * float(n), power_y[-1] * float(n)
        power_x.append(last_x * base_x - last_y * base_y)
        power_y.append(last_x * base_y + last_y * base_x)
    local_x, local_y = [], []
    moment_x = [
        moments[k : k + 1] * ((-1.0) ** (k + 1) / math.factorial(k)) for k in range(ORDER)
    ]
    moment_y = [
        moments[ORDER + k : ORDER + k + 1] * ((-1.0) ** (k + 1) / math.factorial(k))
        for k in range(ORDER)
    ]
    for m in range(ORDER):
        sum_x = jnp.zeros((own, total_lanes), jnp.float32)
        sum_y = jnp.zeros((own, total_lanes), jnp.float32)
        for k in range(ORDER):
            px, py = power_x[m + k], power_y[m + k]
            sum_x = sum_x + (moment_x[k] * px - moment_y[k] * py)
            sum_y = sum_y + (moment_x[k] * py + moment_y[k] * px)
        scale = 1.0 / math.factorial(m)
        local_x.append(jnp.sum(sum_x, axis=1, keepdims=True) * scale)
        local_y.append(jnp.sum(sum_y, axis=1, keepdims=True) * scale)

    own_x, own_y = own_ref[0], own_ref[1]
    field_x = jnp.broadcast_to(local_x[-1], own_x.shape)
    field_y = jnp.broadcast_to(local_y[-1], own_x.shape)
    for m in range(ORDER - 2, -1, -1):
        field_x, field_y = (
            field_x * own_x - field_y * own_y + local_x[m],
            field_x * own_y + field_y * own_x + local_y[m],
        )
    first = (sum_ref[2] - own_y * sum_ref[0] + field_y) * (1.0 / TWO_PI)
    second = (own_x * sum_ref[0] - sum_ref[1] + field_x) * (1.0 / TWO_PI)
    for i in range(side):
        out_ref[0, i] = first[i * side : (i + 1) * side]
        out_ref[1, i] = second[i * side : (i + 1) * side]


def body(particles, near_mask, *, slabs, leaves):
    side, count = particles.shape[1], particles.shape[3]
    own = side * side
    window = side + 2 * WIDTH
    devices = slabs * leaves
    f32 = jnp.float32
    vmem = pl.BlockSpec(memory_space=pltpu.VMEM)
    smem = pl.BlockSpec(memory_space=pltpu.SMEM)
    strips = [
        pltpu.VMEM((3, span(a, side)[1] * span(b, side)[1], count), f32) for a, b in DIRECTIONS
    ]
    bf16 = jnp.bfloat16
    return pl.pallas_call(
        functools.partial(field_kernel, slabs, leaves, side),
        out_shape=jax.ShapeDtypeStruct((2, side, side, count), f32),
        in_specs=[smem, vmem],
        out_specs=vmem,
        scratch_shapes=[
            pltpu.VMEM((3, window * window, count), f32),
            pltpu.VMEM((3, own, count), f32),
            pltpu.VMEM((9, MULTI, 128), f32),
            pltpu.VMEM((devices, 1, 128), f32),
        ] + strips + strips + [
            pltpu.VMEM((MULTI, 128), f32),
            pltpu.VMEM((1, 128), f32),
            pltpu.SemaphoreType.DMA((8,)), pltpu.SemaphoreType.DMA((8,)),
            pltpu.SemaphoreType.DMA((8,)), pltpu.SemaphoreType.DMA((8,)),
            pltpu.SemaphoreType.DMA((devices,)), pltpu.SemaphoreType.DMA((devices,)),
            pltpu.VMEM((count // 128, FEATURES * (window * window + 8), 128), f32),
            pltpu.VMEM((count // 128, FEATURES * (own + 8), 128), f32),
            pltpu.VMEM((count, FEATURES), bf16),
            pltpu.VMEM((window * window, FEATURES, count), bf16),
            pltpu.VMEM((25, 8, count), f32),
            pltpu.VMEM((3, count, 128), f32),
            pltpu.VMEM((3, own, count), f32),
        ],
        compiler_params=pltpu.CompilerParams(
            collective_id=0, has_side_effects=True, vmem_limit_bytes=48 * 1024 * 1024
        ),
        name="field",
    )(near_mask, particles)


def solution(mesh):
    return jax.shard_map(
        functools.partial(body, slabs=mesh.shape["slab"], leaves=mesh.shape["leaf"]),
        mesh=mesh,
        in_specs=(P(None, "slab", "leaf", None), P(None, "slab", "leaf")),
        out_specs=P(None, "slab", "leaf", None),
        check_vma=False,
    )
```

profile of v0, /device:TPU:0, one launch (start us, length us, event | category | flops | bytes accessed | tf_op | source)
XLA Modules:
  0.0 61.6 jit_solution(2329457530783848068)
XLA Ops:
  0.0 0.8 %copy.3.mask_ref = s32[16,4,4]{2,1,0:T(4,128)S(1)} copy(s32[16,4,4]{0,2,1:T(4,128)} %param.3) | data formatting | bytes 2048 | tf_op args[1]
  0.8 0.0 copy-start
  0.8 0.8 %copy-done = f32[3,4,4,256]{3,2,1,0:T(4,128)S(1)} copy-done((f32[3,4,4,256]{3,2,1,0:T(4,128)S(1)}, f32[3,4,4,256]{3,2,1,0:T(4,128)}, u32[]{:S(2)}) %copy-start) | copy-done | bytes 49176
  1.6 59.4 %field.1 = f32[2,4,4,256]{3,2,1,0:T(4,128)S(1)} custom-call(s32[16,4,4]{2,1,0:T(4,128)S(1)} %copy.3.mask_ref, f32[3,4,4,256]{3,2,1,0:T(4,128)S(1)} %copy-done), custom_call_target="tpu_custom_call" | custom-call | tf_op jit(solution)/shard_map/field/pallas_call | solution.py:457
  61.0 0.6 %copy.5 = f32[2,4,4,256]{3,2,1,0:T(4,128)} copy(f32[2,4,4,256]{3,2,1,0:T(4,128)S(1)} %field.1) | data formatting | bytes 65536
Async XLA Ops:
  0.8 0.8 %copy-start = (f32[3,4,4,256]{3,2,1,0:T(4,128)S(1)}, f32[3,4,4,256]{3,2,1,0:T(4,128)}, u32[]{:S(2)}) copy-start(f32[3,4,4,256]{3,2,1,0:T(4,128)} %part_ref.1) | copy-start | bytes 147460
where the time goes:
time: 61.8 us; the launch traced here: 61.6 us
  Pallas kernels  59.4 us (96%)
  local copies, waits for them, and re-layouts  2.21 us (4%)
    pallas_call x1, Pallas kernels, body(): pl.pallas_call(functools.partial(field_kernel, slabs, leaves, side), out_...  59.4 us
    unnamed x4, local copies, waits for them, and re-layouts  2.21 us

commit v1 on v0

--- a/solution.py
+++ b/solution.py
@@ -79,6 +79,17 @@
     ("l1", -2.0, "l1"), ("l1", -2.0, "l2"), ("l2", -2.0, "l1"),
 ]
 ROWS = [(axis, row) for rows in (HIGH, LOW) for axis in (0, 1) for row in rows]
+
+
+def reciprocals(values):
+    out = []
+    for first in range(0, len(values) - 1, 2):
+        a, b = values[first : first + 2]
+        both_inverse = pl.reciprocal(a * b, approx=True)
+        out += [both_inverse * b, both_inverse * a]
+    if len(values) % 2:
+        out.append(pl.reciprocal(values[-1], approx=True))
+    return out
 
 
 def field_kernel(slabs, leaves, side, mask_ref, part_ref, out_ref, *refs):
@@ -249,12 +260,13 @@
             totals = [jnp.zeros((CHUNK, 128), jnp.float32) for _ in range(3)]
             for number, source in enumerate(sources):
                 distance = jnp.dot(left, right_ref[source], preferred_element_type=jnp.float32)
-                inverse = pl.reciprocal(distance, approx=True)
+                inverses = reciprocals(
+                    [distance[:, half * 128 : (half + 1) * 128] for half in range(halves)]
+                )
                 for half in range(halves):
                     lanes = slice(half * 128, (half + 1) * 128)
-                    part = inverse[:, lanes]
                     for q in range(3):
-                        totals[q] = totals[q] + part * gain_ref[number, q : q + 1, lanes]
+                        totals[q] = totals[q] + inverses[half] * gain_ref[number, q : q + 1, lanes]
             for q in range(3):
                 acc_ref[q, pl.ds(at, CHUNK), :] = totals[q]
 

time: 61.8 us -> 59.7 us (0.966)
  Pallas kernels: 59.4 us -> 57.3 us
    pallas_call x1, Pallas kernels: 59.4 us -> 57.3 us  [body(): pl.pallas_call(functools.partial(field_kernel, slabs, leaves, side), out_...]
where the time goes in v1:
time: 59.7 us; the launch traced here: 59.5 us
  Pallas kernels  57.3 us (96%)
  local copies, waits for them, and re-layouts  2.21 us (4%)
    pallas_call x1, Pallas kernels, body(): pl.pallas_call(functools.partial(field_kernel, slabs, leaves, side), out_...  57.3 us
    unnamed x4, local copies, waits for them, and re-layouts  2.21 us

profile of v1, /device:TPU:0, one launch (start us, length us, event | category | flops | bytes accessed | tf_op | source)
XLA Modules:
  0.0 59.5 jit_solution(14284250885738598588)
XLA Ops:
  0.0 0.8 %copy.3.mask_ref = s32[16,4,4]{2,1,0:T(4,128)S(1)} copy(s32[16,4,4]{0,2,1:T(4,128)} %param.3) | data formatting | bytes 2048 | tf_op args[1]
  0.8 0.0 copy-start
  0.8 0.8 %copy-done = f32[3,4,4,256]{3,2,1,0:T(4,128)S(1)} copy-done((f32[3,4,4,256]{3,2,1,0:T(4,128)S(1)}, f32[3,4,4,256]{3,2,1,0:T(4,128)}, u32[]{:S(2)}) %copy-start) | copy-done | bytes 49176
  1.6 57.3 %field.1 = f32[2,4,4,256]{3,2,1,0:T(4,128)S(1)} custom-call(s32[16,4,4]{2,1,0:T(4,128)S(1)} %copy.3.mask_ref, f32[3,4,4,256]{3,2,1,0:T(4,128)S(1)} %copy-done), custom_call_target="tpu_custom_call" | custom-call | tf_op jit(solution)/shard_map/field/pallas_call | solution.py:469
  58.9 0.6 %copy.5 = f32[2,4,4,256]{3,2,1,0:T(4,128)} copy(f32[2,4,4,256]{3,2,1,0:T(4,128)S(1)} %field.1) | data formatting | bytes 65536
Async XLA Ops:
  0.8 0.8 %copy-start = (f32[3,4,4,256]{3,2,1,0:T(4,128)S(1)}, f32[3,4,4,256]{3,2,1,0:T(4,128)}, u32[]{:S(2)}) copy-start(f32[3,4,4,256]{3,2,1,0:T(4,128)} %part_ref.1) | copy-start | bytes 147460

commit v2 on v1

--- a/solution.py
+++ b/solution.py
@@ -97,7 +97,7 @@
     sends, recvs = refs[4:12], refs[12:20]
     multi_ref, row_ref = refs[20:22]
     halo_send, halo_recv, multi_send, multi_recv, row_send, row_recv = refs[22:28]
-    source_ref, target_ref, left_ref, right_ref, gain_ref, acc_ref, sum_ref = refs[28:]
+    source_ref, target_ref, left_ref, right_ref, gain_ref, sum_ref = refs[28:]
     count = slabs * leaves
     window = side + 2 * WIDTH
     own = side * side
@@ -253,10 +253,9 @@
             gain_ref[number, 1:2, :] = strength * (win_ref[0, pl.ds(source, 1), :] + shift_x)
             gain_ref[number, 2:3, :] = strength * (win_ref[1, pl.ds(source, 1), :] + shift_y)
 
-        @pl.loop(0, particles // CHUNK)
-        def _(chunk):
-            at = pl.multiple_of(chunk * CHUNK, CHUNK)
-            left = left_ref[pl.ds(at, CHUNK), :]
+        lines = [[] for _ in range(3)]
+        for at in range(0, particles, CHUNK):
+            left = left_ref[at : at + CHUNK, :]
             totals = [jnp.zeros((CHUNK, 128), jnp.float32) for _ in range(3)]
             for number, source in enumerate(sources):
                 distance = jnp.dot(left, right_ref[source], preferred_element_type=jnp.float32)
@@ -268,16 +267,10 @@
                     for q in range(3):
                         totals[q] = totals[q] + inverses[half] * gain_ref[number, q : q + 1, lanes]
             for q in range(3):
-                acc_ref[q, pl.ds(at, CHUNK), :] = totals[q]
+                lines[q].append(jnp.sum(totals[q].T, axis=0, keepdims=True))
 
         for q in range(3):
-            sums = jnp.concatenate(
-                [
-                    jnp.sum(acc_ref[q, half * 128 : (half + 1) * 128, :].T, axis=0, keepdims=True)
-                    for half in range(halves)
-                ],
-                axis=1,
-            )
+            sums = jnp.concatenate(lines[q], axis=1)
             if first:
                 sum_ref[q, pl.ds(t, 1), :] = sums
             else:
@@ -487,7 +480,6 @@
             pltpu.VMEM((count, FEATURES), bf16),
             pltpu.VMEM((window * window, FEATURES, count), bf16),
             pltpu.VMEM((25, 8, count), f32),
-            pltpu.VMEM((3, count, 128), f32),
             pltpu.VMEM((3, own, count), f32),
         ],
         compiler_params=pltpu.CompilerParams(

time: 59.7 us -> 53.9 us (0.903)
  Pallas kernels: 57.3 us -> 51.5 us
    pallas_call x1, Pallas kernels: 57.3 us -> 51.5 us  [body(): pl.pallas_call(functools.partial(field_kernel, slabs, leaves, side), out_...]
where the time goes in v2:
time: 53.9 us; the launch traced here: 53.7 us
  Pallas kernels  51.5 us (96%)
  local copies, waits for them, and re-layouts  2.21 us (4%)
    pallas_call x1, Pallas kernels, body(): pl.pallas_call(functools.partial(field_kernel, slabs, leaves, side), out_...  51.5 us
    unnamed x4, local copies, waits for them, and re-layouts  2.21 us

profile of v2, /device:TPU:0, one launch (start us, length us, event | category | flops | bytes accessed | tf_op | source)
XLA Modules:
  0.0 53.7 jit_solution(14505112839075886183)
XLA Ops:
  0.0 0.8 %copy.3.mask_ref = s32[16,4,4]{2,1,0:T(4,128)S(1)} copy(s32[16,4,4]{0,2,1:T(4,128)} %param.3) | data formatting | bytes 2048 | tf_op args[1]
  0.8 0.0 copy-start
  0.8 0.8 %copy-done = f32[3,4,4,256]{3,2,1,0:T(4,128)S(1)} copy-done((f32[3,4,4,256]{3,2,1,0:T(4,128)S(1)}, f32[3,4,4,256]{3,2,1,0:T(4,128)}, u32[]{:S(2)}) %copy-start) | copy-done | bytes 49176
  1.6 51.5 %field.1 = f32[2,4,4,256]{3,2,1,0:T(4,128)S(1)} custom-call(s32[16,4,4]{2,1,0:T(4,128)S(1)} %copy.3.mask_ref, f32[3,4,4,256]{3,2,1,0:T(4,128)S(1)} %copy-done), custom_call_target="tpu_custom_call" | custom-call | tf_op jit(solution)/shard_map/field/pallas_call | solution.py:462
  53.1 0.6 %copy.5 = f32[2,4,4,256]{3,2,1,0:T(4,128)} copy(f32[2,4,4,256]{3,2,1,0:T(4,128)S(1)} %field.1) | data formatting | bytes 65536
Async XLA Ops:
  0.8 0.8 %copy-start = (f32[3,4,4,256]{3,2,1,0:T(4,128)S(1)}, f32[3,4,4,256]{3,2,1,0:T(4,128)}, u32[]{:S(2)}) copy-start(f32[3,4,4,256]{3,2,1,0:T(4,128)} %part_ref.1) | copy-start | bytes 147460

commit v3 on v2

--- a/solution.py
+++ b/solution.py
@@ -285,7 +285,7 @@
     fill(target_ref, own_rows, side, True, range(own // 8))
     fill(source_ref, window_rows, window, False, range(WIDTH, WIDTH + side))
 
-    @pl.loop(0, own)
+    @pl.loop(0, own, unroll=8)
     def _(s):
         source_leaf((s // side + WIDTH) * window + lax.rem(s, side) + WIDTH)
 
@@ -322,7 +322,7 @@
 
     fill(source_ref, window_rows, window, False, range(all_leaves // 8))
 
-    @pl.loop(0, all_leaves)
+    @pl.loop(0, all_leaves, unroll=8)
     def _(s):
         source_leaf(s)
 

time: 53.9 us -> 53.3 us (0.989)
  Pallas kernels: 51.5 us -> 50.9 us
    pallas_call x1, Pallas kernels: 51.5 us -> 50.9 us  [body(): pl.pallas_call(functools.partial(field_kernel, slabs, leaves, side), out_...]
where the time goes in v3:
time: 53.3 us; the launch traced here: 53.1 us
  Pallas kernels  50.9 us (95%)
  local copies, waits for them, and re-layouts  2.21 us (4%)
    pallas_call x1, Pallas kernels, body(): pl.pallas_call(functools.partial(field_kernel, slabs, leaves, side), out_...  50.9 us
    unnamed x4, local copies, waits for them, and re-layouts  2.21 us

profile of v3, /device:TPU:0, one launch (start us, length us, event | category | flops | bytes accessed | tf_op | source)
XLA Modules:
  0.0 53.1 jit_solution(12612815634214389658)
XLA Ops:
  0.0 0.8 %copy.3.mask_ref = s32[16,4,4]{2,1,0:T(4,128)S(1)} copy(s32[16,4,4]{0,2,1:T(4,128)} %param.3) | data formatting | bytes 2048 | tf_op args[1]
  0.8 0.0 copy-start
  0.8 0.8 %copy-done = f32[3,4,4,256]{3,2,1,0:T(4,128)S(1)} copy-done((f32[3,4,4,256]{3,2,1,0:T(4,128)S(1)}, f32[3,4,4,256]{3,2,1,0:T(4,128)}, u32[]{:S(2)}) %copy-start) | copy-done | bytes 49176
  1.6 50.9 %field.1 = f32[2,4,4,256]{3,2,1,0:T(4,128)S(1)} custom-call(s32[16,4,4]{2,1,0:T(4,128)S(1)} %copy.3.mask_ref, f32[3,4,4,256]{3,2,1,0:T(4,128)S(1)} %copy-done), custom_call_target="tpu_custom_call" | custom-call | tf_op jit(solution)/shard_map/field/pallas_call | solution.py:462
  52.5 0.6 %copy.5 = f32[2,4,4,256]{3,2,1,0:T(4,128)} copy(f32[2,4,4,256]{3,2,1,0:T(4,128)S(1)} %field.1) | data formatting | bytes 65536
Async XLA Ops:
  0.8 0.8 %copy-start = (f32[3,4,4,256]{3,2,1,0:T(4,128)S(1)}, f32[3,4,4,256]{3,2,1,0:T(4,128)}, u32[]{:S(2)}) copy-start(f32[3,4,4,256]{3,2,1,0:T(4,128)} %part_ref.1) | copy-start | bytes 147460
